TPU v7x, 32 devices: a whole 2x2x4 slice. The times are simulated.
32 devices in a mesh: grp: 2 (over y), re: 16 (over z, x, core).
Axes of the slice: x: 2, y: 2, z: 4, core: 2. Of those that a mesh axis runs over, the one named last changes fastest.
Arguments:
- epmat: bfloat16 [2, 16, 8, 122880], P(None, 're'), may hold values from -0.5 to 0.5
- re_coords: int32 [16, 3], replicated, may hold values from 0 to 15
- rp_coords: int32 [8, 3], replicated, may hold values from 0 to 15
- q_coords: int32 [8, 3], P('grp'), parts along dimension 0, may hold values from 0 to 15
- u_k: bfloat16 [32, 2, 32, 32], P('re'), may hold values from -0.75 to 0.75
- u_kq: bfloat16 [32, 8, 2, 32, 32], P('re', 'grp'), parts along dimension 1, may hold values from -0.75 to 0.75
- evec: bfloat16 [8, 2, 120, 120], P('grp'), parts along dimension 0, may hold values from -0.375 to 0.375
- omega: float32 [8, 120], P('grp'), parts along dimension 0, may hold values from 0.01 to 0.1
- eps_k: float32 [32, 32], replicated, may hold values from -0.3 to 0.3
- eps_kq: float32 [32, 8, 32], P(None, 'grp'), parts along dimension 1, may hold values from -0.3 to 0.3
- temps: float32 [8], replicated, may hold values from 0.005 to 0.05
- owner_states: int32 [32, 16], P('grp'), parts along dimension 0, may hold values from 0 to 4095, as said below
Outputs:
- coupling_sq: bfloat16 [32, 8, 32, 3840], P('re', 'grp'), parts along dimension 1
- rates: float32 [16, 256], P('grp', 're'), parts along dimension 0
There are 2 independent parts, one for each index of `grp`. A program takes and returns all parts, laid end to end along the dimension named above; an argument that names none is the same for every part. Nothing has to cross between parts.
Inputs may be any that keep to these rules, and one draw needn't show every extreme that they name: `owner_states`: row o lists the 16 window states whose terms index o of re owns; state (k-point j, q-point q, band b) has the number (j * 4 + q) * 32 + b and lies on index j // 2. No state appears twice in the array. A row is 8 runs of 2 entries; the states of one run lie on one index, the runs of a row on distinct indices. A quarter of the indices hold a run of every row.
All inputs are finite; a program needn't handle non-finite values.
Results may differ from a plain program's by a relative error of at most 0.0091.
Values may be sent and summed in bfloat16 or wider, within the bound.
A program may use at most 192 MiB of HBM per device.

v0:
```python
import functools

import jax
import jax.numpy as jnp
from jax import lax
from jax.experimental import pallas as pl
from jax.experimental.pallas import tpu as pltpu
from jax.sharding import PartitionSpec as P

GRID = 16
SLOT = 2
LANES = 128


broadening = 0.02


def phase_pair(left_vecs, right_vecs):
    dot_mod = jnp.sum(left_vecs[:, None, :] * right_vecs[None, :, :], axis=2) % GRID
    angles = 2.0 * jnp.pi / GRID * dot_mod.astype(jnp.float32)
    return (jnp.cos(angles).astype(jnp.bfloat16), jnp.sin(angles).astype(jnp.bfloat16))


def fine_points(point_count):
    point_index = jnp.arange(point_count, dtype=jnp.int32)
    return jnp.stack(
        [point_index % GRID, point_index // GRID % GRID, point_index // (GRID * GRID)], axis=1
    )


def pair_rows(first_part, second_part, stack_axis):
    upper = jnp.stack([first_part, second_part], axis=stack_axis)
    lower = jnp.stack([-second_part, first_part], axis=stack_axis)
    return jnp.stack([upper, lower], axis=stack_axis)


def swap_matrix(bands):
    per = LANES // bands
    size = per * LANES
    row = lax.broadcasted_iota(jnp.int32, (size, size), 0)
    col = lax.broadcasted_iota(jnp.int32, (size, size), 1)
    image = (row // bands % per) * LANES + (row // LANES) * bands + row % bands
    return (image == col).astype(jnp.float32).astype(jnp.bfloat16)


def modes_first(x_ref, mix_ref, modes_ref, swap_ref, out_ref, tiles, turned):
    q_count = modes_ref.shape[0]
    bands = out_ref.shape[2] // 2
    per = LANES // bands
    wide = x_ref.shape[2] // bands
    n_tiles = wide // LANES
    pad_tiles = tiles.shape[1]
    groups = bands // per
    out_tiles = out_ref.shape[3] // LANES

    if pad_tiles > n_tiles:
        rest = (bands, pad_tiles - n_tiles, 2 * q_count, LANES)
        tiles[:, n_tiles:] = jnp.zeros(rest, jnp.float32)

    def sum_band(band, carry):
        lanes = pl.ds(pl.multiple_of(band * wide, LANES), wide)
        total = jnp.dot(mix_ref[0], x_ref[0, :, lanes], preferred_element_type=jnp.float32)
        total += jnp.dot(mix_ref[1], x_ref[1, :, lanes], preferred_element_type=jnp.float32)
        for tile in range(n_tiles):
            tiles[band, tile] = total[:, tile * LANES : (tile + 1) * LANES]
        return carry

    lax.fori_loop(0, bands, sum_band, 0)

    for q in range(q_count):
        rows = []
        for part in range(2):
            for group in range(groups):
                rows.append(
                    jnp.concatenate(
                        [
                            tiles[group * per + i, :, part * q_count + q, :].astype(jnp.bfloat16)
                            for i in range(per)
                        ],
                        axis=1,
                    )
                )
        swapped = jnp.dot(
            jnp.concatenate(rows, axis=0), swap_ref[...], preferred_element_type=jnp.float32
        ).astype(jnp.bfloat16)
        stacked = []
        for part in range(2):
            for i in range(per):
                stacked.append(
                    jnp.concatenate(
                        [
                            swapped[
                                (part * groups + group) * pad_tiles : (part * groups + group + 1)
                                * pad_tiles,
                                i * LANES : (i + 1) * LANES,
                            ]
                            for group in range(groups)
                        ],
                        axis=1,
                    )
                )
        moded = jnp.dot(
            modes_ref[q], jnp.concatenate(stacked, axis=0), preferred_element_type=jnp.float32
        ).astype(jnp.bfloat16)
        rows = []
        for part in range(2):
            for group in range(groups):
                rows.append(
                    jnp.concatenate(
                        [
                            moded[
                                (part * per + i) * pad_tiles : (part * per + i + 1) * pad_tiles,
                                group * LANES : (group + 1) * LANES,
                            ]
                            for i in range(per)
                        ],
                        axis=1,
                    )
                )
        back = jnp.dot(
            jnp.concatenate(rows, axis=0), swap_ref[...], preferred_element_type=jnp.float32
        )
        for part in range(2):
            for group in range(groups):
                for i in range(per):
                    turned[part * bands + group * per + i] = back[
                        (part * groups + group) * pad_tiles : (part * groups + group + 1)
                        * pad_tiles,
                        i * LANES : (i + 1) * LANES,
                    ]
        for tile in range(pad_tiles):
            place = tile % out_tiles
            out_ref[tile // out_tiles, q, :, place * LANES : (place + 1) * LANES] = turned[
                :, tile, :
            ].astype(jnp.bfloat16)


def rotate_square(batch, t_ref, cos_ref, sin_ref, one_ref, two_ref, real_ref, imag_ref, out_ref):
    bands = real_ref.shape[1]
    depth, lanes = t_ref.shape
    n_tiles = lanes // LANES
    per = LANES // bands
    row = lax.broadcasted_iota(jnp.int32, (LANES, LANES), 0) // bands
    col = lax.broadcasted_iota(jnp.int32, (LANES, LANES), 1) // bands
    same = row == col
    coeffs = []
    for k in range(batch):
        one = one_ref[k].astype(jnp.float32)
        two = two_ref[k].astype(jnp.float32)
        parts = []
        for tile in range(depth // LANES):
            lane = slice(tile * LANES, (tile + 1) * LANES)
            parts.append((cos_ref[k, :, lane] * one + sin_ref[k, :, lane] * two).astype(jnp.bfloat16))
        coeffs.append(jnp.concatenate(parts, axis=1))
    half = jnp.dot(
        jnp.concatenate(coeffs, axis=0), t_ref[...], preferred_element_type=jnp.float32
    ).astype(jnp.bfloat16)
    for k in range(batch):
        real = jnp.concatenate([real_ref[k].astype(jnp.float32)] * per, axis=0)
        imag = jnp.concatenate([imag_ref[k].astype(jnp.float32)] * per, axis=0)
        real = jnp.where(same, real, 0.0)
        imag = jnp.where(same, imag, 0.0)
        left = jnp.concatenate([real, imag], axis=0)
        right = jnp.concatenate([-imag, real], axis=0)
        both = jnp.concatenate([left, right], axis=1).astype(jnp.bfloat16)
        rows = []
        top = 2 * bands * k
        for tile in range(n_tiles):
            lane = slice(tile * LANES, (tile + 1) * LANES)
            rows.append(
                jnp.concatenate(
                    [half[top : top + bands, lane], half[top + bands : top + 2 * bands, lane]], axis=1
                )
            )
        final = jnp.dot(jnp.concatenate(rows, axis=0), both, preferred_element_type=jnp.float32)
        power = final[:, :LANES] * final[:, :LANES] + final[:, LANES:] * final[:, LANES:]
        power = power.astype(jnp.bfloat16)
        for tile in range(n_tiles):
            out_ref[k, :, tile * LANES : (tile + 1) * LANES] = power[tile * bands : (tile + 1) * bands]


def rate_block(coupling_block, state_ids, eps_k, eps_kq, omega, temps):
    q_count = omega.shape[0]
    band_count = eps_k.shape[1]
    k_index = state_ids // (q_count * band_count)
    q_index = state_ids // band_count % q_count
    n_index = state_ids % band_count
    energy_n = eps_k[k_index, n_index]
    energy_m = eps_kq[k_index, q_index]
    phonon_freq = omega[q_index]
    strength = coupling_block.astype(jnp.float32)
    energy_gap = energy_n[:, None, None] - energy_m[:, None, :]
    peak_scale = broadening / jnp.pi
    lorentz_abs = peak_scale / ((energy_gap + phonon_freq[:, :, None]) ** 2 + broadening**2)
    lorentz_emit = peak_scale / ((energy_gap - phonon_freq[:, :, None]) ** 2 + broadening**2)
    along_mode = jnp.sum(strength * (lorentz_abs + lorentz_emit), axis=2)
    along_band = jnp.sum(strength * (lorentz_abs - lorentz_emit), axis=1)
    base_term = jnp.sum(strength * lorentz_emit, axis=(1, 2))
    bose_occ = 1.0 / jnp.expm1(phonon_freq[None, :, :] / temps[:, None, None])
    fermi_occ = jax.nn.sigmoid(-energy_m[None, :, :] / temps[:, None, None])
    rate_sum = (
        jnp.sum(bose_occ * along_mode[None], axis=2)
        + base_term[None]
        + jnp.sum(fermi_occ * along_band[None], axis=2)
    )
    return rate_sum / (strength.shape[1] * strength.shape[2])


def local(
    epmat,
    re_coords,
    rp_coords,
    q_coords,
    u_k,
    u_kq,
    evec,
    omega,
    eps_k,
    eps_kq,
    temps,
    owner_states,
):
    node_count = lax.axis_size("re")
    self_index = lax.axis_index("re")
    q_count = q_coords.shape[0]
    local_re = epmat.shape[1]
    local_k = u_k.shape[0]
    count_k = local_k * node_count
    bands = u_k.shape[2]
    modes = evec.shape[2]
    wide = modes * bands
    per = LANES // bands
    n_tiles = wide // LANES
    splits = node_count // q_count
    pad_tiles = max(-(-n_tiles // 8) * 8, splits)
    lanes = pad_tiles // splits * LANES
    bf16 = jnp.bfloat16

    cos_q, sin_q = phase_pair(q_coords, rp_coords)
    mix = jnp.stack(
        [jnp.concatenate([cos_q, sin_q], axis=0), jnp.concatenate([-sin_q, cos_q], axis=0)], axis=0
    )
    pad = pad_tiles * per - modes
    padded = jnp.pad(evec, ((0, 0), (0, 0), (0, pad), (0, pad)))
    padded = padded.reshape(q_count, 2, pad_tiles, per, pad_tiles, per)
    padded = padded.transpose(0, 1, 5, 4, 3, 2).reshape(
        q_count, 2, pad_tiles * per, pad_tiles * per
    )
    upper = jnp.concatenate([padded[:, 0], -padded[:, 1]], axis=2)
    lower = jnp.concatenate([padded[:, 1], padded[:, 0]], axis=2)
    mode_mix = jnp.concatenate([upper, lower], axis=1)

    both = jnp.concatenate([u_k[:, None], u_kq], axis=1)
    both = lax.all_gather(both, "re", axis=0, tiled=True)
    rot_k = both[:, 0].transpose(0, 1, 3, 2)
    rot_kq = lax.dynamic_index_in_dim(both, 1 + self_index % q_count, 1, keepdims=False)
    ur, ui = rot_k[:, 0], rot_k[:, 1]
    one = jnp.concatenate(
        [jnp.concatenate([ur, -ui], axis=2), jnp.concatenate([ui, ur], axis=2)], axis=1
    )
    two = jnp.concatenate(
        [jnp.concatenate([-ui, -ur], axis=2), jnp.concatenate([ur, -ui], axis=2)], axis=1
    )
    one = jnp.concatenate([one] * (LANES // (2 * bands)), axis=2)
    two = jnp.concatenate([two] * (LANES // (2 * bands)), axis=2)
    wide_kq = jnp.concatenate([rot_kq] * per, axis=3)
    cos_k, sin_k = phase_pair(fine_points(count_k), re_coords)
    cos_row = jnp.repeat(cos_k.astype(jnp.float32), 2 * bands, axis=1)[:, None, :]
    sin_row = jnp.repeat(sin_k.astype(jnp.float32), 2 * bands, axis=1)[:, None, :]

    call = pl.pallas_call(
        modes_first,
        out_shape=jax.ShapeDtypeStruct((splits, q_count, 2 * bands, lanes), bf16),
        scratch_shapes=[
            pltpu.VMEM((bands, pad_tiles, 2 * q_count, LANES), jnp.float32),
            pltpu.VMEM((2 * bands, pad_tiles, LANES), jnp.float32),
        ],
        compiler_params=pltpu.CompilerParams(vmem_limit_bytes=50 * 2**20),
        name="modes_first",
    )
    swap = swap_matrix(bands)
    sent = [call(epmat[:, r], mix, mode_mix, swap) for r in range(local_re)]
    sent = sent[0][:, :, None] if local_re == 1 else jnp.stack(sent, axis=2)
    sent = sent.reshape(node_count, local_re * 2 * bands, lanes)
    came = lax.all_to_all(sent, "re", split_axis=0, concat_axis=0, tiled=True)
    depth = node_count * local_re * 2 * bands
    came = came.reshape(depth, lanes)

    batch = 4
    power = pl.pallas_call(
        functools.partial(rotate_square, batch),
        grid=(count_k // batch,),
        in_specs=[
            pl.BlockSpec((depth, lanes), lambda i: (0, 0)),
            pl.BlockSpec((batch, 1, depth), lambda i: (i, 0, 0)),
            pl.BlockSpec((batch, 1, depth), lambda i: (i, 0, 0)),
            pl.BlockSpec((batch, 2 * bands, LANES), lambda i: (i, 0, 0)),
            pl.BlockSpec((batch, 2 * bands, LANES), lambda i: (i, 0, 0)),
            pl.BlockSpec((batch, bands, LANES), lambda i: (i, 0, 0)),
            pl.BlockSpec((batch, bands, LANES), lambda i: (i, 0, 0)),
        ],
        out_specs=pl.BlockSpec((batch, bands, lanes), lambda i: (i, 0, 0)),
        out_shape=jax.ShapeDtypeStruct((count_k, bands, lanes), bf16),
        compiler_params=pltpu.CompilerParams(vmem_limit_bytes=50 * 2**20),
        name="rotate_square",
    )(came, cos_row, sin_row, one, two, wide_kq[:, 0], wide_kq[:, 1])

    spread = lax.all_to_all(power, "re", split_axis=0, concat_axis=0, tiled=True)
    spread = spread.reshape(splits, q_count, local_k, bands, lanes)
    coupling = spread.transpose(2, 1, 3, 0, 4).reshape(local_k, q_count, bands, splits * lanes)
    coupling = coupling[..., :wide]

    state_rows = coupling.reshape(-1, wide)
    state_total = state_rows.shape[0]
    capacity = owner_states.shape[1]
    run_count = capacity // SLOT
    runs = owner_states.reshape(node_count, run_count, SLOT)
    holds = runs[:, :, 0] // state_total == self_index
    picked = jnp.sum(jnp.where(holds[:, :, None], runs - self_index * state_total, 0), axis=1)
    picked = picked.reshape(-1)
    strength = state_rows[picked].reshape(-1, modes, bands)
    here = rate_block(
        strength, picked + self_index * state_total, eps_k, eps_kq, omega, temps
    )
    here = here.T.reshape(node_count, 1, SLOT, temps.shape[0])
    placed = jnp.where(holds[:, :, None, None], here, 0.0)
    placed = placed.reshape(node_count, capacity * temps.shape[0])
    rates = lax.psum_scatter(placed, "re", scatter_dimension=0, tiled=True)
    rates = rates.reshape(capacity, temps.shape[0]).T
    return (coupling, rates)


def solution(mesh):
    in_specs = (
        P(None, "re", None, None),
        P(),
        P(),
        P("grp", None),
        P("re", None, None, None),
        P("re", "grp", None, None, None),
        P("grp", None, None, None),
        P("grp", None),
        P(),
        P(None, "grp", None),
        P(),
        P("grp", None),
    )
    out_specs = (P("re", "grp", None, None), P("grp", "re"))
    return jax.shard_map(local, mesh=mesh, in_specs=in_specs, out_specs=out_specs, check_vma=False)
```

profile of v0, /device:TPU:0, one launch (start us, length us, event | category | flops | bytes accessed | tf_op | source)
XLA Modules:
  0.0 280.0 jit_solution(4747295053766491739)
XLA Ops:
  0.6 0.0 copy-start
  0.6 0.8 copy.70
  1.4 0.8 multiply_reduce_fusion.4
  2.2 0.1 fusion.46
  2.3 0.1 cosine_convert_fusion.1
  2.3 1.0 pad.4
  3.3 19.0 %reshape.415 = bf16[4,2,32,4,32,4]{5,4,3,2,1,0:T(8,128)(2,1)} reshape(bf16[4,2,128,128]{3,2,1,0:T(8,128)(2,1)S(1)} %pad.4) | data formatting | bytes 524288 | tf_op jit(solution)/shard_map/reshape | solution.py:245
  22.3 15.7 %copy.71 = bf16[4,2,4,32,4,32]{5,4,3,2,0,1:T(4,128)(2,1)S(1)} copy(bf16[4,2,4,32,4,32]{2,3,4,5,1,0:T(8,128)(2,1)} %bitcast.60) | data formatting | bytes 524288 | tf_op jit(solution)/shard_map/transpose | solution.py:246
  38.0 0.5 reshape.416
  38.7 0.1 maximum_maximum_fusion.modes_ref
  38.7 1.0 convert_convert_fusion.swap_ref
  39.7 20.2 %modes_first.1 = bf16[4,4,64,1024]{3,2,1,0:T(8,128)(2,1)} custom-call(bf16[2,8,122880]{2,1,0:T(8,128)(2,1)} %bitcast.63, bf16[2,8,8]{2,1,0:T(8,128)(2,1)S(1)} %pad_maximum_fusion.2.mix_ref, bf16[4,256,256]{2,1,0:T(8,128)(2,1)S(1)} %maximum_maximum_fusion.modes_ref, bf16[512,512]{1,0:T(8,128)(2,1)S(1)} %convert_convert_fusion.swap_ref), custom_call_target="tpu_custom_call" | custom-call | tf_op jit(solution)/shard_map/modes_first/pallas_call | solution.py:282
  59.9 7.7 %all-to-all-start = ((bf16[16,64,1024]{2,1,0:T(8,128)(2,1)}), bf16[16,64,1024]{2,1,0:T(8,128)(2,1)}, u32[]{:S(2)}, u32[]{:S(2)}) async-start(bf16[16,64,1024]{2,1,0:T(8,128)(2,1)} %bitcast.8), calls=%async_computation | async-start | bytes 4194304 | tf_op jit(solution)/shard_map/all_to_all | solution.py:285
  67.6 0.0 copy-done.6
  67.6 0.1 multiply_reduce_fusion.3
  67.7 0.1 fusion.19
  67.8 0.1 copy.72
  67.9 0.1 broadcast_in_dim.35
  68.0 0.2 broadcast_in_dim_reshape.6.cos_ref
  68.2 0.1 copy.73
  68.3 0.1 broadcast_in_dim.36
  68.4 0.2 broadcast_in_dim_reshape.7.sin_ref
  68.6 0.0 copy-done.3
  68.6 0.1 copy.75
  68.7 0.0 copy-done.4
  68.7 0.1 copy.74
  68.9 68.1 %all_gather.3 = bf16[32,5,2,32,32]{3,4,0,2,1:T(8,128)(2,1)S(1)} all-gather(bf16[2,5,2,32,32]{3,4,0,2,1:T(8,128)(2,1)S(1)} %pad_maximum_fusion.1), channel_id=1, replica_groups=mesh['grp'=2,'re'=16] {'re'}, dimensions={0}, use_global_device_ids=true | all-gather | bytes 696320 | tf_op jit(solution)/shard_map/all_gather | solution.py:254
  137.0 0.1 constant_dynamic-slice_fusion
  137.1 0.3 copy.76
  137.4 0.6 pad_maximum_fusion
  138.0 0.1 fusion.43
  138.1 1.1 maximum_maximum_fusion.2
  139.3 0.0 all-to-all-done
  139.3 9.7 %rotate_square.1 = bf16[32,32,1024]{2,1,0:T(8,128)(2,1)} custom-call(bf16[1024,1024]{1,0:T(8,128)(2,1)} %bitcast.9.t_ref, f32[32,1,1024]{2,1,0:T(1,128)S(1)} %broadcast_in_dim_reshape.6.cos_ref, f32[32,1,1024]{2,1,0:T(1,128)S(1)} %broadcast_in_dim_reshape.7.sin_ref, bf16[32,64,128]{2,1,0:T(8,128)(2,1)S(1)} %get-tuple-element.28.one_ref, ...), custom_call_target="tpu_custom_call" | custom-call | tf_op jit(solution)/shard_map/rotate_square/pallas_call | solution.py:290
  149.0 7.6 %all-to-all-start.1 = ((bf16[32,32,1024]{2,1,0:T(8,128)(2,1)}), bf16[32,32,1024]{2,1,0:T(8,128)(2,1)S(1)}, u32[]{:S(2)}, u32[]{:S(2)}) async-start(bf16[32,32,1024]{2,1,0:T(8,128)(2,1)} %rotate_square.1), calls=%async_computation.1 | async-start | bytes 4194304 | tf_op jit(solution)/shard_map/all_to_all | solution.py:308
  156.7 0.0 copy-done.5
  156.7 0.1 copy.78
  156.9 0.1 copy.79
  156.9 0.1 reshape.421
  157.1 0.0 copy-done.2
  157.1 0.6 gather_fusion
  157.7 0.7 gather_fusion.3
  158.4 0.7 gather_fusion.2
  159.1 0.0 copy-done.8
  159.1 0.6 dynamic-slice
  159.7 0.1 fusion.47
  159.8 38.0 %all-to-all-done.1 = bf16[32,32,1024]{2,1,0:T(8,128)(2,1)S(1)} async-done(((bf16[32,32,1024]{2,1,0:T(8,128)(2,1)}), bf16[32,32,1024]{2,1,0:T(8,128)(2,1)S(1)}, u32[]{:S(2)}, u32[]{:S(2)}) %all-to-all-start.1) | async-done | bytes 2097184 | tf_op jit(solution)/shard_map/all_to_all | solution.py:308
  197.8 3.0 %copy.77 = bf16[2,4,32,4,1024]{4,3,2,1,0:T(4,128)(2,1)} copy(bf16[2,4,32,4,1024]{4,2,0,1,3:T(8,128)(2,1)S(1)} %bitcast.61) | data formatting | bytes 4194304 | tf_op jit(solution)/shard_map/transpose | solution.py:310
  200.8 3.3 %reshape.419 = bf16[2,4,32,4096]{3,2,1,0:T(8,128)(2,1)S(1)} reshape(bf16[2,4,32,4,1024]{4,3,2,1,0:T(4,128)(2,1)} %copy.77) | data formatting | bytes 4194304 | tf_op jit(solution)/shard_map/reshape | solution.py:310
  204.0 1.4 slice.53
  205.5 2.7 gather_fusion.1
  208.2 0.0 copy-start.7
  208.2 0.6 reshape.424
  208.8 0.5 copy.80
  209.3 0.8 multiply_reduce_fusion.1
  210.2 0.0 copy-done.7
  210.2 0.2 fusion.11
  210.4 0.2 fusion.12
  210.6 0.1 copy.83
  210.7 0.1 copy.84
  210.8 67.7 %all-reduce.1 = f32[16,128]{0,1:T(8,128)S(1)} all-reduce(f32[16,128]{0,1:T(8,128)S(1)} %bitcast.65), channel_id=2, replica_groups=mesh['grp'=2,'re'=16] {'re'}, use_global_device_ids=true, to_apply=%region_8.9.clone | all-reduce | flops 2048 | bytes 16384
  278.5 0.8 dynamic-slice_reduce_fusion
  279.3 0.1 reshape.423
  279.4 0.7 copy.85
  (35 shorter events, 0.4 us)
Async XLA Ops:
  0.6 157.0 %copy-start = (f32[32,4,32]{2,1,0:T(4,128)S(1)}, f32[32,4,32]{2,1,0:T(4,128)}, u32[]{:S(2)}) copy-start(f32[32,4,32]{2,1,0:T(4,128)} %param.21) | copy-start | bytes 49156
  59.9 7.7 %copy-start.6 = (s32[16,3]{0,1:T(4,128)S(1)}, s32[16,3]{0,1:T(4,128)}, u32[]{:S(2)}) copy-start(s32[16,3]{0,1:T(4,128)} %param.13) | copy-start | bytes 580
  59.9 8.7 %copy-start.3 = (bf16[2,4,2,32,32]{4,3,2,1,0:T(8,128)(2,1)S(1)}, bf16[2,4,2,32,32]{4,3,2,1,0:T(8,128)(2,1)}, u32[]{:S(2)}) copy-start(bf16[2,4,2,32,32]{4,3,2,1,0:T(8,128)(2,1)} %param.17) | copy-start | bytes 98308
  59.9 8.8 %copy-start.4 = (bf16[2,2,32,32]{3,2,1,0:T(8,128)(2,1)S(1)}, bf16[2,2,32,32]{3,2,1,0:T(8,128)(2,1)}, u32[]{:S(2)}) copy-start(bf16[2,2,32,32]{3,2,1,0:T(8,128)(2,1)} %param.16) | copy-start | bytes 24580
  59.9 79.4 %all-to-all-start = ((bf16[16,64,1024]{2,1,0:T(8,128)(2,1)}), bf16[16,64,1024]{2,1,0:T(8,128)(2,1)}, u32[]{:S(2)}, u32[]{:S(2)}) async-start(bf16[16,64,1024]{2,1,0:T(8,128)(2,1)} %bitcast.8), calls=%async_computation | async-start | bytes 4194304 | tf_op jit(solution)/shard_map/all_to_all | solution.py:285
  149.0 7.7 %copy-start.5 = (s32[16,16]{1,0:T(8,128)S(1)}, s32[16,16]{1,0:T(8,128)}, u32[]{:S(2)}) copy-start(s32[16,16]{1,0:T(8,128)} %param.23) | copy-start | bytes 3076
  149.0 8.1 %copy-start.2 = (f32[4,120]{1,0:T(4,128)S(1)}, f32[4,120]{1,0:T(4,128)}, u32[]{:S(2)}) copy-start(f32[4,120]{1,0:T(4,128)} %param.19) | copy-start | bytes 5764
  149.0 9.3 %copy-start.1 = (f32[32,32]{1,0:T(8,128)S(1)}, f32[32,32]{1,0:T(8,128)}, u32[]{:S(2)}) copy-start(f32[32,32]{1,0:T(8,128)} %param.20) | copy-start | bytes 12292
  149.0 10.0 %copy-start.8 = (u32[32]{0:T(128)S(1)}, u32[32]{0:T(128)}, u32[]{:S(2)}) copy-start(u32[32]{0:T(128)} %constant.227) | copy-start | bytes 388
  149.0 48.8 %all-to-all-start.1 = ((bf16[32,32,1024]{2,1,0:T(8,128)(2,1)}), bf16[32,32,1024]{2,1,0:T(8,128)(2,1)S(1)}, u32[]{:S(2)}, u32[]{:S(2)}) async-start(bf16[32,32,1024]{2,1,0:T(8,128)(2,1)} %rotate_square.1), calls=%async_computation.1 | async-start | bytes 4194304 | tf_op jit(solution)/shard_map/all_to_all | solution.py:308
  208.2 2.0 copy-start.7
where the time goes:
time: 281 us; the launch traced here: 280 us
  blocking collectives  136 us (48%)
  local copies, waits for them, and re-layouts  54.5 us (19%)
  waiting for transfers between devices  38 us (14%)
  Pallas kernels  29.9 us (11%)
  starting transfers between devices  15.3 us (5%)
  other arithmetic  5.43 us (2%)
    all_gather x1, blocking collectives, local(): both = lax.all_gather(both, 're', axis=0, tiled=True)  68.1 us
    unnamed x1, blocking collectives  67.7 us
    all_to_all x1, waiting for transfers between devices, local(): lax.all_to_all(power, 're', split_axis=0, concat_axis=0, tiled=True)  38 us
    pallas_call x1, Pallas kernels, local(): sent = [call(epmat[:, r], mix, mode_mix, swap) for r in range(local_re)]  20.2 us
    reshape x1, local copies, waits for them, and re-layouts, local(): padded = padded.reshape(q_count, 2, pad_tiles, per, pad_tiles, per)  19 us
    transpose x1, local copies, waits for them, and re-layouts, local(): padded.transpose(0, 1, 5, 4, 3, 2)  15.7 us
    pallas_call x1, Pallas kernels, local(): pl.pallas_call(functools.partial(rotate_square, batch), grid=(count_k //...  9.72 us
    all_to_all x1, starting transfers between devices, local(): came = lax.all_to_all(sent, 're', split_axis=0, concat_axis=0, tiled=True)  7.67 us
  transfers between devices with their start and end apart: 2, of which 1 were waited for; matrix products, arithmetic and copies ran while one was open for 2% of the time, Pallas kernels for 0%

commit v1 on v0

v1 whole, which is shorter than its diff:
```python
import functools

import jax
import jax.numpy as jnp
import numpy as np
from jax import lax
from jax.experimental import pallas as pl
from jax.experimental.pallas import tpu as pltpu
from jax.sharding import PartitionSpec as P

GRID = 16
SLOT = 2
LANES = 128


broadening = 0.02


def phase_pair(left_vecs, right_vecs):
    dot_mod = jnp.sum(left_vecs[:, None, :] * right_vecs[None, :, :], axis=2) % GRID
    angles = 2.0 * jnp.pi / GRID * dot_mod.astype(jnp.float32)
    return (jnp.cos(angles).astype(jnp.bfloat16), jnp.sin(angles).astype(jnp.bfloat16))


def fine_points(point_count):
    point_index = jnp.arange(point_count, dtype=jnp.int32)
    return jnp.stack(
        [point_index % GRID, point_index // GRID % GRID, point_index // (GRID * GRID)], axis=1
    )


def pair_rows(first_part, second_part, stack_axis):
    upper = jnp.stack([first_part, second_part], axis=stack_axis)
    lower = jnp.stack([-second_part, first_part], axis=stack_axis)
    return jnp.stack([upper, lower], axis=stack_axis)


MESH = pl.DeviceIdType.MESH


def swap_matrix(bands):
    per = LANES // bands
    row = np.arange(per * LANES)
    image = (row // bands % per) * LANES + (row // LANES) * bands + row % bands
    return jnp.asarray(np.eye(per * LANES)[image], jnp.bfloat16)


def mode_order(modes, per, pad_tiles):
    row = np.arange(per * pad_tiles)
    source = (row % pad_tiles) * per + row // pad_tiles
    return jnp.asarray(source[:, None] == np.arange(modes)[None, :], jnp.bfloat16)


def widen_matrix(bands):
    per = LANES // bands
    out = np.zeros((LANES, 5 * LANES))
    plans = [
        [(0, 1), (1, -1)] * (per // 2),
        [(1, 1), (0, 1)] * (per // 2),
        [(1, -1), (0, -1)] * (per // 2),
        [(2, 1)] * per,
        [(3, 1)] * per,
    ]
    for tile, plan in enumerate(plans):
        for place, (source, sign) in enumerate(plan):
            for band in range(bands):
                out[source * bands + band, tile * LANES + place * bands + band] = sign
    return jnp.asarray(out, jnp.bfloat16)


def exchange(
    node_count,
    local_k,
    batch,
    x_ref,
    mix_ref,
    evec_ref,
    packs_ref,
    cos_ref,
    sin_ref,
    swap_ref,
    order_ref,
    widen_ref,
    out_ref,
    tiles,
    turned,
    staged,
    gathered,
    packs,
    power,
    pack_send,
    pack_recv,
    mode_send,
    mode_recv,
    power_send,
    power_recv,
    own_sem,
):
    q_count = evec_ref.shape[0]
    bands = packs_ref.shape[2]
    per = LANES // bands
    wide = x_ref.shape[2] // bands
    n_tiles = wide // LANES
    pad_tiles = tiles.shape[1]
    groups = bands // per
    lanes = staged.shape[3]
    out_tiles = lanes // LANES
    splits = staged.shape[0]
    depth = node_count * 2 * bands

    me = lax.axis_index("re")
    my_q = lax.rem(me, q_count)
    my_split = me // q_count

    barrier = pltpu.get_barrier_semaphore()

    def greet(i, carry):
        other = lax.rem(me + i, node_count)
        pl.semaphore_signal(barrier, inc=1, device_id={"re": other}, device_id_type=MESH)
        return carry

    lax.fori_loop(1, node_count, greet, 0)
    pl.semaphore_wait(barrier, node_count - 1)

    def pack_copy(to):
        return pltpu.make_async_remote_copy(
            src_ref=packs_ref.at[lax.rem(to, q_count)],
            dst_ref=packs.at[me],
            send_sem=pack_send.at[to],
            recv_sem=pack_recv.at[me],
            device_id={"re": to},
            device_id_type=MESH,
        )

    def pack_from(source):
        return pltpu.make_async_remote_copy(
            src_ref=packs_ref.at[0],
            dst_ref=packs.at[source],
            send_sem=pack_send.at[source],
            recv_sem=pack_recv.at[source],
            device_id={"re": source},
            device_id_type=MESH,
        )

    def send_pack(i, carry):
        pack_copy(lax.rem(me + i, node_count)).start()
        return carry

    lax.fori_loop(1, node_count, send_pack, 0)
    packs[me] = packs_ref[my_q]

    if pad_tiles > n_tiles:
        rest = (bands, pad_tiles - n_tiles, 2 * q_count, LANES)
        tiles[:, n_tiles:] = jnp.zeros(rest, jnp.float32)

    def sum_band(band, carry):
        at = pl.ds(pl.multiple_of(band * wide, LANES), wide)
        total = jnp.dot(mix_ref[0], x_ref[0, :, at], preferred_element_type=jnp.float32)
        total += jnp.dot(mix_ref[1], x_ref[1, :, at], preferred_element_type=jnp.float32)
        for tile in range(n_tiles):
            tiles[band, tile] = total[:, tile * LANES : (tile + 1) * LANES]
        return carry

    lax.fori_loop(0, bands, sum_band, 0)

    def mode_copy(split, step):
        to = split * q_count + lax.rem(me + step, q_count)
        return to, pltpu.make_async_remote_copy(
            src_ref=staged.at[split, step],
            dst_ref=gathered.at[me],
            send_sem=mode_send.at[to],
            recv_sem=mode_recv.at[me],
            device_id={"re": to},
            device_id_type=MESH,
        )

    def mode_from(source):
        return pltpu.make_async_remote_copy(
            src_ref=staged.at[0, 0],
            dst_ref=gathered.at[source],
            send_sem=mode_send.at[source],
            recv_sem=mode_recv.at[source],
            device_id={"re": source},
            device_id_type=MESH,
        )

    nt = (((1,), (1,)), ((), ()))
    for q in range(q_count):
        q_at = lax.rem(me + q, q_count)
        ordered = []
        for part in range(2):
            first = lax.dot_general(
                order_ref[...], evec_ref[q_at, part], nt, preferred_element_type=jnp.float32
            ).astype(jnp.bfloat16)
            ordered.append(
                lax.dot_general(first, order_ref[...], nt, preferred_element_type=jnp.float32)
            )
        mode_mix = jnp.concatenate(
            [
                jnp.concatenate([ordered[0], -ordered[1]], axis=1),
                jnp.concatenate([ordered[1], ordered[0]], axis=1),
            ],
            axis=0,
        ).astype(jnp.bfloat16)
        rows = []
        for part in range(2):
            for group in range(groups):
                rows.append(
                    jnp.concatenate(
                        [
                            tiles[group * per + i, :, part * q_count + q, :].astype(jnp.bfloat16)
                            for i in range(per)
                        ],
                        axis=1,
                    )
                )
        swapped = jnp.dot(
            jnp.concatenate(rows, axis=0), swap_ref[...], preferred_element_type=jnp.float32
        ).astype(jnp.bfloat16)
        stacked = []
        for part in range(2):
            for i in range(per):
                stacked.append(
                    jnp.concatenate(
                        [
                            swapped[
                                (part * groups + group) * pad_tiles : (part * groups + group + 1)
                                * pad_tiles,
                                i * LANES : (i + 1) * LANES,
                            ]
                            for group in range(groups)
                        ],
                        axis=1,
                    )
                )
        moded = jnp.dot(
            mode_mix, jnp.concatenate(stacked, axis=0), preferred_element_type=jnp.float32
        ).astype(jnp.bfloat16)
        rows = []
        for part in range(2):
            for group in range(groups):
                rows.append(
                    jnp.concatenate(
                        [
                            moded[
                                (part * per + i) * pad_tiles : (part * per + i + 1) * pad_tiles,
                                group * LANES : (group + 1) * LANES,
                            ]
                            for i in range(per)
                        ],
                        axis=1,
                    )
                )
        back = jnp.dot(
            jnp.concatenate(rows, axis=0), swap_ref[...], preferred_element_type=jnp.float32
        )
        for part in range(2):
            for group in range(groups):
                for i in range(per):
                    turned[part * bands + group * per + i] = back[
                        (part * groups + group) * pad_tiles : (part * groups + group + 1)
                        * pad_tiles,
                        i * LANES : (i + 1) * LANES,
                    ]
        for tile in range(pad_tiles):
            place = tile % out_tiles
            staged[tile // out_tiles, q, :, place * LANES : (place + 1) * LANES] = turned[
                :, tile, :
            ].astype(jnp.bfloat16)

        def send_modes(split, carry):
            to, copy = mode_copy(split, q)

            @pl.when(to != me)
            def _():
                copy.start()

            return carry

        lax.fori_loop(0, splits, send_modes, 0)
    gathered[me] = staged[my_split, 0]

    def arrivals(i, carry):
        source = lax.rem(me + i, node_count)
        pack_from(source).wait_recv()
        mode_from(source).wait_recv()
        return carry

    lax.fori_loop(1, node_count, arrivals, 0)

    row = lax.broadcasted_iota(jnp.int32, (LANES, LANES), 0) // bands
    col = lax.broadcasted_iota(jnp.int32, (LANES, LANES), 1) // bands
    same = row == col
    nodes = batch // local_k
    place = pl.ds(pl.multiple_of(my_split * lanes, LANES), lanes)

    def power_copy(to):
        return pltpu.make_async_remote_copy(
            src_ref=power.at[pl.ds(to * local_k, local_k)],
            dst_ref=out_ref.at[:, my_q, :, place],
            send_sem=power_send.at[to],
            recv_sem=power_recv.at[me],
            device_id={"re": to},
            device_id_type=MESH,
        )

    def power_from(source):
        at = pl.ds(pl.multiple_of(source // q_count * lanes, LANES), lanes)
        return pltpu.make_async_remote_copy(
            src_ref=power.at[pl.ds(0, local_k)],
            dst_ref=out_ref.at[:, lax.rem(source, q_count), :, at],
            send_sem=power_send.at[source],
            recv_sem=power_recv.at[source],
            device_id={"re": source},
            device_id_type=MESH,
        )

    own_copy = pltpu.make_async_copy(
        power.at[pl.ds(me * local_k, local_k)], out_ref.at[:, my_q, :, place], own_sem
    )

    def rotate(i, carry):
        node = lax.rem(me // nodes + i + 1, node_count // nodes) * nodes
        base = node * local_k
        pack = jnp.concatenate(
            [packs[node + k // local_k, k % local_k] for k in range(batch)], axis=0
        )
        spread = jnp.dot(pack, widen_ref[...], preferred_element_type=jnp.float32)
        spread = [
            [spread[k * bands : (k + 1) * bands, t * LANES : (t + 1) * LANES] for t in range(5)]
            for k in range(batch)
        ]
        coeffs = []
        for k in range(batch):
            one = jnp.concatenate([spread[k][0], spread[k][1]], axis=0)
            two = jnp.concatenate([spread[k][2], spread[k][0]], axis=0)
            parts = []
            for tile in range(depth // LANES):
                lane = slice(tile * LANES, (tile + 1) * LANES)
                value = cos_ref[base + k, :, lane] * one + sin_ref[base + k, :, lane] * two
                parts.append(value.astype(jnp.bfloat16))
            coeffs.append(jnp.concatenate(parts, axis=1))
        half = jnp.dot(
            jnp.concatenate(coeffs, axis=0),
            gathered[...].reshape(depth, lanes),
            preferred_element_type=jnp.float32,
        ).astype(jnp.bfloat16)
        for k in range(batch):
            real = jnp.where(same, jnp.concatenate([spread[k][3]] * per, axis=0), 0.0)
            imag = jnp.where(same, jnp.concatenate([spread[k][4]] * per, axis=0), 0.0)
            both = jnp.concatenate(
                [
                    jnp.concatenate([real, -imag], axis=1),
                    jnp.concatenate([imag, real], axis=1),
                ],
                axis=0,
            ).astype(jnp.bfloat16)
            rows = []
            top = 2 * bands * k
            for tile in range(out_tiles):
                lane = slice(tile * LANES, (tile + 1) * LANES)
                rows.append(
                    jnp.concatenate(
                        [half[top : top + bands, lane], half[top + bands : top + 2 * bands, lane]],
                        axis=1,
                    )
                )
            final = jnp.dot(jnp.concatenate(rows, axis=0), both, preferred_element_type=jnp.float32)
            square = final[:, :LANES] * final[:, :LANES] + final[:, LANES:] * final[:, LANES:]
            square = square.astype(jnp.bfloat16)
            for tile in range(out_tiles):
                power[base + k, :, tile * LANES : (tile + 1) * LANES] = square[
                    tile * bands : (tile + 1) * bands
                ]
        for n in range(nodes):
            to = node + n

            @pl.when(to != me)
            def _():
                power_copy(to).start()

            @pl.when(to == me)
            def _():
                own_copy.start()

        return carry

    lax.fori_loop(0, node_count // nodes, rotate, 0)

    def finish(i, carry):
        other = lax.rem(me + i, node_count)
        pack_copy(other).wait_send()
        mode_from(other).wait_send()
        power_copy(other).wait_send()
        power_from(other).wait_recv()
        return carry

    lax.fori_loop(1, node_count, finish, 0)
    own_copy.wait()


def hand_over(node_count, value_ref, out_ref, came, send_sem, recv_sem):
    me = lax.axis_index("re")
    barrier = pltpu.get_barrier_semaphore()

    def greet(i, carry):
        other = lax.rem(me + i, node_count)
        pl.semaphore_signal(barrier, inc=1, device_id={"re": other}, device_id_type=MESH)
        return carry

    lax.fori_loop(1, node_count, greet, 0)
    pl.semaphore_wait(barrier, node_count - 1)

    def copy(to, slot):
        return pltpu.make_async_remote_copy(
            src_ref=value_ref.at[to],
            dst_ref=came.at[slot],
            send_sem=send_sem.at[to],
            recv_sem=recv_sem.at[slot],
            device_id={"re": to},
            device_id_type=MESH,
        )

    def send(i, carry):
        copy(lax.rem(me + i, node_count), me).start()
        return carry

    lax.fori_loop(1, node_count, send, 0)
    came[me] = value_ref[me]

    def finish(i, carry):
        other = lax.rem(me + i, node_count)
        copy(other, other).wait()
        return carry

    lax.fori_loop(1, node_count, finish, 0)
    out_ref[...] = jnp.sum(came[...], axis=0)


def rate_block(coupling_block, state_ids, eps_k, eps_kq, omega, temps):
    q_count = omega.shape[0]
    band_count = eps_k.shape[1]
    k_index = state_ids // (q_count * band_count)
    q_index = state_ids // band_count % q_count
    n_index = state_ids % band_count
    energy_n = eps_k[k_index, n_index]
    energy_m = eps_kq[k_index, q_index]
    phonon_freq = omega[q_index]
    strength = coupling_block.astype(jnp.float32)
    energy_gap = energy_n[:, None, None] - energy_m[:, None, :]
    peak_scale = broadening / jnp.pi
    lorentz_abs = peak_scale / ((energy_gap + phonon_freq[:, :, None]) ** 2 + broadening**2)
    lorentz_emit = peak_scale / ((energy_gap - phonon_freq[:, :, None]) ** 2 + broadening**2)
    along_mode = jnp.sum(strength * (lorentz_abs + lorentz_emit), axis=2)
    along_band = jnp.sum(strength * (lorentz_abs - lorentz_emit), axis=1)
    base_term = jnp.sum(strength * lorentz_emit, axis=(1, 2))
    bose_occ = 1.0 / jnp.expm1(phonon_freq[None, :, :] / temps[:, None, None])
    fermi_occ = jax.nn.sigmoid(-energy_m[None, :, :] / temps[:, None, None])
    rate_sum = (
        jnp.sum(bose_occ * along_mode[None], axis=2)
        + base_term[None]
        + jnp.sum(fermi_occ * along_band[None], axis=2)
    )
    return rate_sum / (strength.shape[1] * strength.shape[2])


def local(
    epmat,
    re_coords,
    rp_coords,
    q_coords,
    u_k,
    u_kq,
    evec,
    omega,
    eps_k,
    eps_kq,
    temps,
    owner_states,
):
    node_count = lax.axis_size("re")
    self_index = lax.axis_index("re")
    q_count = q_coords.shape[0]
    local_k = u_k.shape[0]
    count_k = local_k * node_count
    bands = u_k.shape[2]
    modes = evec.shape[2]
    wide = modes * bands
    per = LANES // bands
    n_tiles = wide // LANES
    splits = node_count // q_count
    pad_tiles = max(-(-n_tiles // 8) * 8, splits)
    lanes = pad_tiles // splits * LANES
    bf16 = jnp.bfloat16

    own_q = q_coords[(jnp.arange(q_count) + self_index) % q_count]
    cos_q, sin_q = phase_pair(own_q, rp_coords)
    mix = jnp.stack(
        [jnp.concatenate([cos_q, sin_q], axis=0), jnp.concatenate([-sin_q, cos_q], axis=0)], axis=0
    )
    cos_k, sin_k = phase_pair(fine_points(count_k), re_coords)
    cos_row = jnp.repeat(cos_k.astype(jnp.float32), 2 * bands, axis=1)[:, None, :]
    sin_row = jnp.repeat(sin_k.astype(jnp.float32), 2 * bands, axis=1)[:, None, :]
    depth = node_count * 2 * bands

    turned_k = u_k.transpose(0, 1, 3, 2)
    packs = jnp.stack(
        [
            jnp.concatenate([turned_k[:, 0], turned_k[:, 1], u_kq[:, q, 0], u_kq[:, q, 1]], axis=2)
            for q in range(q_count)
        ],
        axis=0,
    )

    batch = 2 * local_k
    dma = pltpu.SemaphoreType.DMA
    vmem = pl.BlockSpec(memory_space=pltpu.VMEM)
    power = pl.pallas_call(
        functools.partial(exchange, node_count, local_k, batch),
        in_specs=[vmem] * 9,
        out_specs=pl.BlockSpec(memory_space=pl.ANY),
        out_shape=jax.ShapeDtypeStruct((local_k, q_count, bands, splits * lanes), bf16),
        scratch_shapes=[
            pltpu.VMEM((bands, pad_tiles, 2 * q_count, LANES), jnp.float32),
            pltpu.VMEM((2 * bands, pad_tiles, LANES), jnp.float32),
            pltpu.VMEM((splits, q_count, 2 * bands, lanes), bf16),
            pltpu.VMEM((node_count, 2 * bands, lanes), bf16),
            pltpu.VMEM((node_count, local_k, bands, LANES), bf16),
            pltpu.VMEM((count_k, bands, lanes), bf16),
        ]
        + [dma((node_count,))] * 6
        + [dma],
        compiler_params=pltpu.CompilerParams(
            vmem_limit_bytes=56 * 2**20, collective_id=0, has_side_effects=True
        ),
        name="exchange",
    )(
        epmat[:, 0],
        mix,
        evec,
        packs,
        cos_row,
        sin_row,
        swap_matrix(bands),
        mode_order(modes, per, pad_tiles),
        widen_matrix(bands),
    )
    coupling = power[..., :wide]

    state_rows = coupling.reshape(-1, wide)
    state_total = state_rows.shape[0]
    capacity = owner_states.shape[1]
    run_count = capacity // SLOT
    runs = owner_states.reshape(node_count, run_count, SLOT)
    holds = runs[:, :, 0] // state_total == self_index
    picked = jnp.sum(jnp.where(holds[:, :, None], runs - self_index * state_total, 0), axis=1)
    picked = picked.reshape(-1)
    strength = state_rows[picked].reshape(-1, modes, bands)
    here = rate_block(
        strength, picked + self_index * state_total, eps_k, eps_kq, omega, temps
    )
    here = here.T.reshape(node_count, 1, SLOT, temps.shape[0])
    placed = jnp.where(holds[:, :, None, None], here, 0.0)
    placed = placed.reshape(node_count, capacity * temps.shape[0])
    width = -(-placed.shape[1] // (8 * LANES)) * 8 * LANES
    placed = jnp.pad(placed, ((0, 0), (0, width - placed.shape[1])))
    placed = placed.reshape(node_count, width // LANES, LANES)
    rates = pl.pallas_call(
        functools.partial(hand_over, node_count),
        in_specs=[vmem],
        out_specs=vmem,
        out_shape=jax.ShapeDtypeStruct(placed.shape[1:], jnp.float32),
        scratch_shapes=[pltpu.VMEM(placed.shape, jnp.float32)] + [dma((node_count,))] * 2,
        compiler_params=pltpu.CompilerParams(collective_id=1, has_side_effects=True),
        name="hand_over",
    )(placed)
    rates = rates.reshape(-1)[: capacity * temps.shape[0]]
    rates = rates.reshape(capacity, temps.shape[0]).T
    return (coupling, rates)


def solution(mesh):
    in_specs = (
        P(None, "re", None, None),
        P(),
        P(),
        P("grp", None),
        P("re", None, None, None),
        P("re", "grp", None, None, None),
        P("grp", None, None, None),
        P("grp", None),
        P(),
        P(None, "grp", None),
        P(),
        P("grp", None),
    )
    out_specs = (P("re", "grp", None, None), P("grp", "re"))
    return jax.shard_map(local, mesh=mesh, in_specs=in_specs, out_specs=out_specs, check_vma=False)
```

time: 281 us -> 143 us (0.51)
  blocking collectives: 136 us -> 0 us
  Pallas kernels: 29.9 us -> 121 us
  local copies, waits for them, and re-layouts: 54.5 us -> 16.2 us
  waiting for transfers between devices: 38 us -> 0 us
  starting transfers between devices: 15.3 us -> 0 us
    pallas_call x2, Pallas kernels: 29.9 us -> 121 us  [the longest x1 98.2 us: local(): pl.pallas_call(functools.partial(exchange, node_count, local_k, batch), i...]
    all_gather x1 -> x0, blocking collectives: 68.1 us -> none  [local(): both = lax.all_gather(both, 're', axis=0, tiled=True)]
    unnamed x1 -> x0, blocking collectives: 67.7 us -> none
    all_to_all x2 -> x0, waiting for transfers between devices: 38 us -> none  [the longest x1 38 us: local(): lax.all_to_all(power, 're', split_axis=0, concat_axis=0, tiled=True)]
    reshape x3 -> x1, local copies, waits for them, and re-layouts: 22.7 us -> 0.79 us  [local(): placed = placed.reshape(node_count, width // LANES, LANES)]
    transpose x2 -> x0, local copies, waits for them, and re-layouts: 18.7 us -> none  [the longest x1 15.7 us: local(): padded.transpose(0, 1, 5, 4, 3, 2)]
    all_to_all x2 -> x0, starting transfers between devices: 15.3 us -> none  [the longest x1 7.67 us: local(): came = lax.all_to_all(sent, 're', split_axis=0, concat_axis=0, tiled=True)]
    convert_element_type x2, local copies, waits for them, and re-layouts: 1.09 us -> 3.95 us  [rate_block(): strength = coupling_block.astype(jnp.float32)]
  transfers between devices with their start and end apart: 2 -> 0, of which waited for: 1 -> 0; matrix products, arithmetic and copies ran while one was open for 2% -> 0% of each run, Pallas kernels for 0% -> 0%
where the time goes in v1:
time: 143 us
  Pallas kernels  121 us (85%)
  local copies, waits for them, and re-layouts  16.2 us (11%)
  other arithmetic  4.62 us (3%)
    pallas_call x1, Pallas kernels, local(): pl.pallas_call(functools.partial(exchange, node_count, local_k, batch), i...  98.2 us
    pallas_call x1, Pallas kernels, local(): pl.pallas_call(functools.partial(hand_over, node_count), in_specs=[vmem],...  22.7 us
    convert_element_type x2, local copies, waits for them, and re-layouts, rate_block(): strength = coupling_block.astype(jnp.float32)  3.95 us

profile of v1, /device:TPU:0, one launch (start us, length us, event | category | flops | bytes accessed | tf_op | source)
XLA Modules:
  0.0 142.6 jit_solution(11301629311965661820)
XLA Ops:
  0.6 0.0 copy-start
  0.6 0.9 slice_bitcast_fusion.7
  1.5 0.8 copy.98
  2.4 0.1 maximum_bitcast_fusion
  2.5 0.1 maximum_bitcast_fusion.1
  2.6 0.6 pad_maximum_fusion.packs_ref
  3.2 1.2 gather_fusion
  4.5 0.1 copy.97
  4.6 0.8 multiply_reduce_fusion.4
  5.4 0.1 fusion.32
  5.4 0.1 cosine_convert_fusion.1
  5.5 0.6 pad_maximum_fusion.2.mix_ref
  6.1 0.8 multiply_reduce_fusion.3
  6.9 0.1 fusion.14
  6.9 0.1 copy.107
  7.0 0.1 broadcast_in_dim.33
  7.2 0.8 broadcast_in_dim_reshape.6.cos_ref
  8.0 0.1 copy.108
  8.1 0.1 broadcast_in_dim.34
  8.2 0.8 broadcast_in_dim_reshape.7.sin_ref
  9.0 98.2 %exchange.1 = bf16[2,4,32,4096]{3,2,1,0:T(8,128)(2,1)} custom-call(bf16[2,8,122880]{2,1,0:T(8,128)(2,1)} %bitcast.72, bf16[2,8,8]{2,1,0:T(8,128)(2,1)} %pad_maximum_fusion.2.mix_ref, bf16[4,2,120,120]{3,2,1,0:T(8,128)(2,1)} %evec_ref.1, bf16[4,2,32,128]{3,2,1,0:T(8,128)(2,1)} %pad_maximum_fusion.packs_ref, f32[32,1,1024]{2,1,0:T(1,128)} %broadcast_in_dim_reshape.6.cos_ref, ...), custom_call_target="tpu_custom_call" | custom-call | tf_op jit(solution)/shard_map/exchange/pallas_call | solution.py:518
  107.3 0.0 copy-start.4
  107.3 1.7 %slice.56 = bf16[2,4,32,3840]{3,2,1,0:T(8,128)(2,1)S(1)} slice(bf16[2,4,32,4096]{3,2,1,0:T(8,128)(2,1)} %exchange.1), slice={[0:2], [0:4], [0:32], [0:3840]} | slice | bytes 3932160 | tf_op jit(solution)/shard_map/slice | solution.py:548
  109.0 0.0 copy-start.3
  109.0 0.0 copy-done.4
  109.0 0.1 copy.109
  109.2 0.1 copy.110
  109.2 0.1 reshape.456
  109.4 0.7 gather_fusion.2
  110.1 0.0 copy-start.1
  110.1 1.9 %reshape.460 = f32[32,120,32]{2,1,0:T(8,128)} reshape(bf16[32,3840]{1,0:T(8,128)(2,1)S(1)} %gather_fusion.2) | data formatting | bytes 737280 | tf_op jit(solution)/shard_map/convert_element_type | solution.py:449
  112.0 0.0 copy-done.3
  112.0 0.0 copy-start.2
  112.0 0.0 copy-start.5
  112.0 2.1 %copy.111 = f32[32,120,32]{1,2,0:T(8,128)S(1)} copy(f32[32,120,32]{2,1,0:T(8,128)} %reshape.460) | data formatting | bytes 983040 | tf_op jit(solution)/shard_map/convert_element_type | solution.py:449
  114.1 0.0 copy-done
  114.1 0.7 gather_fusion.4
  114.8 0.0 copy-done.1
  114.8 0.7 gather_fusion.3
  115.5 0.1 fusion.33
  115.6 0.0 copy-done.2
  115.6 0.6 gather_fusion.1
  116.2 0.8 multiply_reduce_fusion.1
  117.0 0.0 copy-done.5
  117.0 0.2 fusion.6
  117.2 0.2 fusion.7
  117.4 0.1 copy.114
  117.5 0.1 copy.115
  117.7 0.8 copy.118.value_ref
  118.5 22.7 %hand_over.1 = f32[8,128]{1,0:T(8,128)} custom-call(f32[16,8,128]{2,1,0:T(8,128)} %copy.118.value_ref), custom_call_target="tpu_custom_call" | custom-call | tf_op jit(solution)/shard_map/hand_over/pallas_call | solution.py:568
  141.2 0.7 slice_reduce_fusion
  141.9 0.1 reshape.459
  141.9 0.7 copy.117
  (19 shorter events, 0.3 us)
Async XLA Ops:
  0.6 113.5 %copy-start = (f32[32,4,32]{2,1,0:T(4,128)S(1)}, f32[32,4,32]{2,1,0:T(4,128)}, u32[]{:S(2)}) copy-start(f32[32,4,32]{2,1,0:T(4,128)} %param.24) | copy-start | bytes 49156
  107.3 1.7 %copy-start.4 = (s32[16,16]{1,0:T(8,128)S(1)}, s32[16,16]{1,0:T(8,128)}, u32[]{:S(2)}) copy-start(s32[16,16]{1,0:T(8,128)} %param.26) | copy-start | bytes 3076
  109.0 3.0 %copy-start.3 = (bf16[2,4,32,3840]{3,2,1,0:T(8,128)(2,1)}, bf16[2,4,32,3840]{3,2,1,0:T(8,128)(2,1)S(1)}, u32[]{:S(2)}) copy-start(bf16[2,4,32,3840]{3,2,1,0:T(8,128)(2,1)S(1)} %slice.56) | copy-start | bytes 5898244
  110.1 4.7 %copy-start.1 = (f32[32,32]{1,0:T(8,128)S(1)}, f32[32,32]{1,0:T(8,128)}, u32[]{:S(2)}) copy-start(f32[32,32]{1,0:T(8,128)} %param.23) | copy-start | bytes 12292
  112.0 3.6 %copy-start.2 = (f32[4,120]{1,0:T(4,128)S(1)}, f32[4,120]{1,0:T(4,128)}, u32[]{:S(2)}) copy-start(f32[4,120]{1,0:T(4,128)} %param.22) | copy-start | bytes 5764
  112.0 5.0 %copy-start.5 = (f32[8]{0:T(128)S(1)}, f32[8]{0:T(128)}, u32[]{:S(2)}) copy-start(f32[8]{0:T(128)} %param.25) | copy-start | bytes 100

commit v2 on v1

--- a/solution.py
+++ b/solution.py
@@ -99,7 +99,7 @@
     q_count = evec_ref.shape[0]
     bands = packs_ref.shape[2]
     per = LANES // bands
-    wide = x_ref.shape[2] // bands
+    wide = x_ref.shape[3] // bands
     n_tiles = wide // LANES
     pad_tiles = tiles.shape[1]
     groups = bands // per
@@ -107,10 +107,26 @@
     out_tiles = lanes // LANES
     splits = staged.shape[0]
     depth = node_count * 2 * bands
+    parts = 2 if out_tiles % 2 == 0 else 1
+    part_tiles = out_tiles // parts
 
     me = lax.axis_index("re")
     my_q = lax.rem(me, q_count)
     my_split = me // q_count
+
+    def sized(split, part, act):
+        start = split * out_tiles + part * part_tiles
+        rest = n_tiles % part_tiles
+
+        @pl.when(start + part_tiles <= n_tiles)
+        def _():
+            act(part_tiles * LANES)
+
+        if rest:
+
+            @pl.when(start == n_tiles - rest)
+            def _():
+                act(rest * LANES)
 
     barrier = pltpu.get_barrier_semaphore()
 
@@ -155,34 +171,48 @@
 
     def sum_band(band, carry):
         at = pl.ds(pl.multiple_of(band * wide, LANES), wide)
-        total = jnp.dot(mix_ref[0], x_ref[0, :, at], preferred_element_type=jnp.float32)
-        total += jnp.dot(mix_ref[1], x_ref[1, :, at], preferred_element_type=jnp.float32)
+        total = jnp.dot(mix_ref[0], x_ref[0, 0, :, at], preferred_element_type=jnp.float32)
+        total += jnp.dot(mix_ref[1], x_ref[1, 0, :, at], preferred_element_type=jnp.float32)
         for tile in range(n_tiles):
             tiles[band, tile] = total[:, tile * LANES : (tile + 1) * LANES]
         return carry
 
     lax.fori_loop(0, bands, sum_band, 0)
 
-    def mode_copy(split, step):
-        to = split * q_count + lax.rem(me + step, q_count)
-        return to, pltpu.make_async_remote_copy(
-            src_ref=staged.at[split, step],
-            dst_ref=gathered.at[me],
-            send_sem=mode_send.at[to],
-            recv_sem=mode_recv.at[me],
+    def mode_copy(to, step, part, width):
+        lane = pl.ds(part * part_tiles * LANES, width)
+        return pltpu.make_async_remote_copy(
+            src_ref=staged.at[to // q_count, step, :, lane],
+            dst_ref=gathered.at[me, :, lane],
+            send_sem=mode_send.at[part, to],
+            recv_sem=mode_recv.at[part, me],
             device_id={"re": to},
             device_id_type=MESH,
         )
 
-    def mode_from(source):
+    def mode_from(source, part, width):
+        lane = pl.ds(part * part_tiles * LANES, width)
         return pltpu.make_async_remote_copy(
-            src_ref=staged.at[0, 0],
-            dst_ref=gathered.at[source],
-            send_sem=mode_send.at[source],
-            recv_sem=mode_recv.at[source],
+            src_ref=staged.at[0, 0, :, lane],
+            dst_ref=gathered.at[source, :, lane],
+            send_sem=mode_send.at[part, source],
+            recv_sem=mode_recv.at[part, source],
             device_id={"re": source},
             device_id_type=MESH,
         )
+
+    def send_modes(step, part):
+        def body(i, carry):
+            split = lax.rem(my_split + i, splits)
+            to = split * q_count + lax.rem(me + step, q_count)
+
+            @pl.when(to != me)
+            def _():
+                sized(split, part, lambda width: mode_copy(to, step, part, width).start())
+
+            return carry
+
+        lax.fori_loop(0, splits, body, 0)
 
     nt = (((1,), (1,)), ((), ()))
     for q in range(q_count):
@@ -268,58 +298,58 @@
                 :, tile, :
             ].astype(jnp.bfloat16)
 
-        def send_modes(split, carry):
-            to, copy = mode_copy(split, q)
-
-            @pl.when(to != me)
-            def _():
-                copy.start()
-
-            return carry
-
-        lax.fori_loop(0, splits, send_modes, 0)
+        send_modes(q, 0)
+    for part in range(1, parts):
+        for q in range(q_count):
+            send_modes(q, part)
     gathered[me] = staged[my_split, 0]
 
-    def arrivals(i, carry):
-        source = lax.rem(me + i, node_count)
-        pack_from(source).wait_recv()
-        mode_from(source).wait_recv()
-        return carry
-
-    lax.fori_loop(1, node_count, arrivals, 0)
+    def packs_in(i, carry):
+        pack_from(lax.rem(me + i, node_count)).wait_recv()
+        return carry
+
+    lax.fori_loop(1, node_count, packs_in, 0)
 
     row = lax.broadcasted_iota(jnp.int32, (LANES, LANES), 0) // bands
     col = lax.broadcasted_iota(jnp.int32, (LANES, LANES), 1) // bands
     same = row == col
     nodes = batch // local_k
-    place = pl.ds(pl.multiple_of(my_split * lanes, LANES), lanes)
-
-    def power_copy(to):
+
+    def power_copy(to, part, width):
+        at = pl.multiple_of(my_split * lanes + part * part_tiles * LANES, LANES)
         return pltpu.make_async_remote_copy(
-            src_ref=power.at[pl.ds(to * local_k, local_k)],
-            dst_ref=out_ref.at[:, my_q, :, place],
-            send_sem=power_send.at[to],
-            recv_sem=power_recv.at[me],
+            src_ref=power.at[
+                pl.ds(to * local_k, local_k), :, pl.ds(part * part_tiles * LANES, width)
+            ],
+            dst_ref=out_ref.at[:, my_q, :, pl.ds(at, width)],
+            send_sem=power_send.at[part, to],
+            recv_sem=power_recv.at[part, me],
             device_id={"re": to},
             device_id_type=MESH,
         )
 
-    def power_from(source):
-        at = pl.ds(pl.multiple_of(source // q_count * lanes, LANES), lanes)
+    def power_from(source, part, width):
+        at = source // q_count * lanes + part * part_tiles * LANES
+        at = pl.multiple_of(at, LANES)
         return pltpu.make_async_remote_copy(
-            src_ref=power.at[pl.ds(0, local_k)],
-            dst_ref=out_ref.at[:, lax.rem(source, q_count), :, at],
-            send_sem=power_send.at[source],
-            recv_sem=power_recv.at[source],
+            src_ref=power.at[pl.ds(0, local_k), :, pl.ds(part * part_tiles * LANES, width)],
+            dst_ref=out_ref.at[:, lax.rem(source, q_count), :, pl.ds(at, width)],
+            send_sem=power_send.at[part, source],
+            recv_sem=power_recv.at[part, source],
             device_id={"re": source},
             device_id_type=MESH,
         )
 
-    own_copy = pltpu.make_async_copy(
-        power.at[pl.ds(me * local_k, local_k)], out_ref.at[:, my_q, :, place], own_sem
-    )
-
-    def rotate(i, carry):
+    def own_copy(part, width):
+        at = pl.multiple_of(my_split * lanes + part * part_tiles * LANES, LANES)
+        return pltpu.make_async_copy(
+            power.at[pl.ds(me * local_k, local_k), :, pl.ds(part * part_tiles * LANES, width)],
+            out_ref.at[:, my_q, :, pl.ds(at, width)],
+            own_sem.at[part],
+        )
+
+    def rotate(part, i, carry):
+        low = part * part_tiles * LANES
         node = lax.rem(me // nodes + i + 1, node_count // nodes) * nodes
         base = node * local_k
         pack = jnp.concatenate(
@@ -342,7 +372,7 @@
             coeffs.append(jnp.concatenate(parts, axis=1))
         half = jnp.dot(
             jnp.concatenate(coeffs, axis=0),
-            gathered[...].reshape(depth, lanes),
+            gathered[:, :, low : low + part_tiles * LANES].reshape(depth, part_tiles * LANES),
             preferred_element_type=jnp.float32,
         ).astype(jnp.bfloat16)
         for k in range(batch):
@@ -357,7 +387,7 @@
             ).astype(jnp.bfloat16)
             rows = []
             top = 2 * bands * k
-            for tile in range(out_tiles):
+            for tile in range(part_tiles):
                 lane = slice(tile * LANES, (tile + 1) * LANES)
                 rows.append(
                     jnp.concatenate(
@@ -368,35 +398,45 @@
             final = jnp.dot(jnp.concatenate(rows, axis=0), both, preferred_element_type=jnp.float32)
             square = final[:, :LANES] * final[:, :LANES] + final[:, LANES:] * final[:, LANES:]
             square = square.astype(jnp.bfloat16)
-            for tile in range(out_tiles):
-                power[base + k, :, tile * LANES : (tile + 1) * LANES] = square[
-                    tile * bands : (tile + 1) * bands
-                ]
+            for tile in range(part_tiles):
+                lane = slice(low + tile * LANES, low + (tile + 1) * LANES)
+                power[base + k, :, lane] = square[tile * bands : (tile + 1) * bands]
         for n in range(nodes):
             to = node + n
 
             @pl.when(to != me)
             def _():
-                power_copy(to).start()
+                sized(my_split, part, lambda width: power_copy(to, part, width).start())
 
             @pl.when(to == me)
             def _():
-                own_copy.start()
-
-        return carry
-
-    lax.fori_loop(0, node_count // nodes, rotate, 0)
+                sized(my_split, part, lambda width: own_copy(part, width).start())
+
+        return carry
+
+    for part in range(parts):
+
+        def modes_in(i, carry):
+            source = lax.rem(me + i, node_count)
+            sized(my_split, part, lambda width: mode_from(source, part, width).wait_recv())
+            return carry
+
+        lax.fori_loop(1, node_count, modes_in, 0)
+        lax.fori_loop(0, node_count // nodes, functools.partial(rotate, part), 0)
 
     def finish(i, carry):
         other = lax.rem(me + i, node_count)
+        split = other // q_count
         pack_copy(other).wait_send()
-        mode_from(other).wait_send()
-        power_copy(other).wait_send()
-        power_from(other).wait_recv()
+        for part in range(parts):
+            sized(split, part, lambda width: mode_from(other, part, width).wait_send())
+            sized(my_split, part, lambda width: power_copy(other, part, width).wait_send())
+            sized(split, part, lambda width: power_from(other, part, width).wait_recv())
         return carry
 
     lax.fori_loop(1, node_count, finish, 0)
-    own_copy.wait()
+    for part in range(parts):
+        sized(my_split, part, lambda width: own_copy(part, width).wait())
 
 
 def hand_over(node_count, value_ref, out_ref, came, send_sem, recv_sem):
@@ -515,11 +555,11 @@
     batch = 2 * local_k
     dma = pltpu.SemaphoreType.DMA
     vmem = pl.BlockSpec(memory_space=pltpu.VMEM)
-    power = pl.pallas_call(
+    coupling = pl.pallas_call(
         functools.partial(exchange, node_count, local_k, batch),
         in_specs=[vmem] * 9,
         out_specs=pl.BlockSpec(memory_space=pl.ANY),
-        out_shape=jax.ShapeDtypeStruct((local_k, q_count, bands, splits * lanes), bf16),
+        out_shape=jax.ShapeDtypeStruct((local_k, q_count, bands, wide), bf16),
         scratch_shapes=[
             pltpu.VMEM((bands, pad_tiles, 2 * q_count, LANES), jnp.float32),
             pltpu.VMEM((2 * bands, pad_tiles, LANES), jnp.float32),
@@ -528,14 +568,15 @@
             pltpu.VMEM((node_count, local_k, bands, LANES), bf16),
             pltpu.VMEM((count_k, bands, lanes), bf16),
         ]
-        + [dma((node_count,))] * 6
-        + [dma],
+        + [dma((node_count,))] * 2
+        + [dma((2, node_count))] * 4
+        + [dma((2,))],
         compiler_params=pltpu.CompilerParams(
             vmem_limit_bytes=56 * 2**20, collective_id=0, has_side_effects=True
         ),
         name="exchange",
     )(
-        epmat[:, 0],
+        epmat,
         mix,
         evec,
         packs,
@@ -545,7 +586,6 @@
         mode_order(modes, per, pad_tiles),
         widen_matrix(bands),
     )
-    coupling = power[..., :wide]
 
     state_rows = coupling.reshape(-1, wide)
     state_total = state_rows.shape[0]

time: 143 us -> 136 us (0.951)
  Pallas kernels: 121 us -> 115 us
    pallas_call x1, Pallas kernels: 22.7 us -> 15.5 us  [local(): pl.pallas_call(functools.partial(hand_over, node_count), in_specs=[vmem],...]
    convert_element_type x2, local copies, waits for them, and re-layouts: 3.95 us -> 1.1 us  [rate_block(): strength = coupling_block.astype(jnp.float32)]
    gather x1, local copies, waits for them, and re-layouts: 0.7 us -> 2.73 us  [local(): strength = state_rows[picked].reshape(-1, modes, bands)]
    slice x1 -> x0, local copies, waits for them, and re-layouts: 1.68 us -> none  [local(): coupling = power[..., :wide]]
    pallas_call x1, Pallas kernels: 98.2 us -> 99.7 us  [local(): pl.pallas_call(functools.partial(exchange, node_count, local_k, batch), i...]
    unnamed x16 -> x17, local copies, waits for them, and re-layouts: 1.63 us -> 2.9 us
where the time goes in v2:
time: 136 us
  Pallas kernels  115 us (85%)
  local copies, waits for them, and re-layouts  15 us (11%)
  other arithmetic  4.62 us (3%)
    pallas_call x1, Pallas kernels, local(): pl.pallas_call(functools.partial(exchange, node_count, local_k, batch), i...  99.7 us
    pallas_call x1, Pallas kernels, local(): pl.pallas_call(functools.partial(hand_over, node_count), in_specs=[vmem],...  15.5 us
    unnamed x17, local copies, waits for them, and re-layouts  2.9 us
    gather x1, local copies, waits for them, and re-layouts, local(): strength = state_rows[picked].reshape(-1, modes, bands)  2.73 us

profile of v2, /device:TPU:0, one launch (start us, length us, event | category | flops | bytes accessed | tf_op | source)
XLA Modules:
  0.0 135.7 jit_solution(16693006199433182882)
XLA Ops:
  0.6 0.0 copy-start
  0.6 0.9 slice_bitcast_fusion.7
  1.5 0.8 copy.98
  2.4 0.1 maximum_bitcast_fusion
  2.5 0.1 maximum_bitcast_fusion.1
  2.6 0.6 pad_maximum_fusion.packs_ref
  3.2 1.2 gather_fusion
  4.5 0.1 copy.97
  4.6 0.8 multiply_reduce_fusion.4
  5.4 0.1 fusion.32
  5.4 0.1 cosine_convert_fusion.1
  5.5 0.6 pad_maximum_fusion.2.mix_ref
  6.1 0.8 multiply_reduce_fusion.3
  6.9 0.1 fusion.14
  7.0 0.1 copy.107
  7.0 0.1 broadcast_in_dim.33
  7.2 0.8 broadcast_in_dim_reshape.6.cos_ref
  8.0 0.1 copy.108
  8.1 0.1 broadcast_in_dim.34
  8.2 0.8 broadcast_in_dim_reshape.7.sin_ref
  9.0 0.0 copy-start.4
  9.0 99.7 %exchange.1 = bf16[2,4,32,3840]{3,2,1,0:T(8,128)(2,1)} custom-call(bf16[2,1,8,122880]{3,2,1,0:T(8,128)(2,1)} %x_ref.1, bf16[2,8,8]{2,1,0:T(8,128)(2,1)} %pad_maximum_fusion.2.mix_ref, bf16[4,2,120,120]{3,2,1,0:T(8,128)(2,1)} %evec_ref.1, bf16[4,2,32,128]{3,2,1,0:T(8,128)(2,1)} %pad_maximum_fusion.packs_ref, f32[32,1,1024]{2,1,0:T(1,128)} %broadcast_in_dim_reshape.6.cos_ref, ...), custom_call_target="tpu_custom_call" | custom-call | tf_op jit(solution)/shard_map/exchange/pallas_call | solution.py:558
  108.7 0.0 copy-done.4
  108.7 0.1 copy.109
  108.9 0.1 copy.110
  109.0 0.1 reshape.456
  109.1 2.7 %gather_fusion.2 = bf16[32,3840]{1,0:T(8,128)(2,1)S(1)} fusion(bf16[256,3840]{1,0:T(8,128)(2,1)} %bitcast.70, s32[1024]{0:T(1024)S(1)} %pad_clamp_fusion), kind=kCustom, calls=%fused_computation.2 | custom fusion | bytes 491648 | tf_op jit(solution)/shard_map/gather | solution.py:598
  111.9 0.0 copy-start.2
  111.9 0.6 reshape.460
  112.5 0.0 copy-start.3
  112.5 0.0 copy-start.5
  112.5 0.5 copy.111
  113.0 0.0 copy-start.1
  113.0 0.0 copy-done
  113.0 0.7 gather_fusion.4
  113.7 0.0 copy-done.2
  113.7 0.7 gather_fusion.3
  114.4 0.1 fusion.33
  114.5 0.0 copy-done.3
  114.5 0.6 gather_fusion.1
  115.1 0.8 multiply_reduce_fusion.1
  115.9 0.0 copy-done.5
  115.9 0.2 fusion.7
  116.1 0.2 fusion.6
  116.4 0.1 copy.114
  116.4 0.1 copy.115
  116.6 0.8 copy.118.value_ref
  117.4 15.5 %hand_over.1 = f32[8,128]{1,0:T(8,128)} custom-call(f32[16,8,128]{2,1,0:T(8,128)} %copy.118.value_ref), custom_call_target="tpu_custom_call" | custom-call | tf_op jit(solution)/shard_map/hand_over/pallas_call | solution.py:608
  132.9 0.7 slice_reduce_fusion
  133.6 0.1 reshape.459
  133.7 0.7 copy.117
  134.4 0.0 copy-done.1
  134.4 1.3 copy.131
  (19 shorter events, 0.3 us)
Async XLA Ops:
  0.6 112.4 %copy-start = (f32[32,4,32]{2,1,0:T(4,128)S(1)}, f32[32,4,32]{2,1,0:T(4,128)}, u32[]{:S(2)}) copy-start(f32[32,4,32]{2,1,0:T(4,128)} %param.24) | copy-start | bytes 49156
  9.0 99.7 %copy-start.4 = (s32[16,16]{1,0:T(8,128)S(1)}, s32[16,16]{1,0:T(8,128)}, u32[]{:S(2)}) copy-start(s32[16,16]{1,0:T(8,128)} %param.26) | copy-start | bytes 3076
  111.9 1.8 %copy-start.2 = (f32[32,32]{1,0:T(8,128)S(1)}, f32[32,32]{1,0:T(8,128)}, u32[]{:S(2)}) copy-start(f32[32,32]{1,0:T(8,128)} %param.23) | copy-start | bytes 12292
  112.5 2.1 %copy-start.3 = (f32[4,120]{1,0:T(4,128)S(1)}, f32[4,120]{1,0:T(4,128)}, u32[]{:S(2)}) copy-start(f32[4,120]{1,0:T(4,128)} %param.22) | copy-start | bytes 5764
  112.5 3.4 %copy-start.5 = (f32[8]{0:T(128)S(1)}, f32[8]{0:T(128)}, u32[]{:S(2)}) copy-start(f32[8]{0:T(128)} %param.25) | copy-start | bytes 100
  113.0 21.4 %copy-start.1 = (bf16[2,4,32,3840]{3,2,1,0:T(8,128)(2,1)S(1)}, bf16[2,4,32,3840]{3,2,1,0:T(8,128)(2,1)}, u32[]{:S(2)}) copy-start(bf16[2,4,32,3840]{3,2,1,0:T(8,128)(2,1)} %exchange.1) | copy-start | bytes 5898244

commit v3 on v2

--- a/solution.py
+++ b/solution.py
@@ -76,8 +76,7 @@
     mix_ref,
     evec_ref,
     packs_ref,
-    cos_ref,
-    sin_ref,
+    wave_ref,
     swap_ref,
     order_ref,
     widen_ref,
@@ -169,15 +168,17 @@
         rest = (bands, pad_tiles - n_tiles, 2 * q_count, LANES)
         tiles[:, n_tiles:] = jnp.zeros(rest, jnp.float32)
 
-    def sum_band(band, carry):
-        at = pl.ds(pl.multiple_of(band * wide, LANES), wide)
-        total = jnp.dot(mix_ref[0], x_ref[0, 0, :, at], preferred_element_type=jnp.float32)
-        total += jnp.dot(mix_ref[1], x_ref[1, 0, :, at], preferred_element_type=jnp.float32)
-        for tile in range(n_tiles):
-            tiles[band, tile] = total[:, tile * LANES : (tile + 1) * LANES]
-        return carry
-
-    lax.fori_loop(0, bands, sum_band, 0)
+    def sum_bands(group, carry):
+        for i in range(per):
+            band = group * per + i
+            at = pl.ds(pl.multiple_of(band * wide, LANES), wide)
+            total = jnp.dot(mix_ref[0], x_ref[0, 0, :, at], preferred_element_type=jnp.float32)
+            total += jnp.dot(mix_ref[1], x_ref[1, 0, :, at], preferred_element_type=jnp.float32)
+            for tile in range(n_tiles):
+                tiles[band, tile] = total[:, tile * LANES : (tile + 1) * LANES]
+        return carry
+
+    lax.fori_loop(0, groups, sum_bands, 0)
 
     def mode_copy(to, step, part, width):
         lane = pl.ds(part * part_tiles * LANES, width)
@@ -364,10 +365,11 @@
         for k in range(batch):
             one = jnp.concatenate([spread[k][0], spread[k][1]], axis=0)
             two = jnp.concatenate([spread[k][2], spread[k][0]], axis=0)
+            wave = wave_ref[base + k]
             parts = []
             for tile in range(depth // LANES):
                 lane = slice(tile * LANES, (tile + 1) * LANES)
-                value = cos_ref[base + k, :, lane] * one + sin_ref[base + k, :, lane] * two
+                value = wave[0:1, lane] * one + wave[1:2, lane] * two
                 parts.append(value.astype(jnp.bfloat16))
             coeffs.append(jnp.concatenate(parts, axis=1))
         half = jnp.dot(
@@ -533,14 +535,15 @@
     lanes = pad_tiles // splits * LANES
     bf16 = jnp.bfloat16
 
-    own_q = q_coords[(jnp.arange(q_count) + self_index) % q_count]
+    twice = jnp.concatenate([q_coords, q_coords], axis=0)
+    own_q = lax.dynamic_slice_in_dim(twice, self_index % q_count, q_count, 0)
     cos_q, sin_q = phase_pair(own_q, rp_coords)
     mix = jnp.stack(
         [jnp.concatenate([cos_q, sin_q], axis=0), jnp.concatenate([-sin_q, cos_q], axis=0)], axis=0
     )
     cos_k, sin_k = phase_pair(fine_points(count_k), re_coords)
-    cos_row = jnp.repeat(cos_k.astype(jnp.float32), 2 * bands, axis=1)[:, None, :]
-    sin_row = jnp.repeat(sin_k.astype(jnp.float32), 2 * bands, axis=1)[:, None, :]
+    waves = jnp.stack([cos_k, sin_k], axis=1).astype(jnp.float32)
+    waves = jnp.repeat(waves, 2 * bands, axis=2)
     depth = node_count * 2 * bands
 
     turned_k = u_k.transpose(0, 1, 3, 2)
@@ -557,7 +560,7 @@
     vmem = pl.BlockSpec(memory_space=pltpu.VMEM)
     coupling = pl.pallas_call(
         functools.partial(exchange, node_count, local_k, batch),
-        in_specs=[vmem] * 9,
+        in_specs=[vmem] * 8,
         out_specs=pl.BlockSpec(memory_space=pl.ANY),
         out_shape=jax.ShapeDtypeStruct((local_k, q_count, bands, wide), bf16),
         scratch_shapes=[
@@ -580,8 +583,7 @@
         mix,
         evec,
         packs,
-        cos_row,
-        sin_row,
+        waves,
         swap_matrix(bands),
         mode_order(modes, per, pad_tiles),
         widen_matrix(bands),

time: 136 us -> 132 us (0.971)
  Pallas kernels: 115 us -> 112 us
  local copies, waits for them, and re-layouts: 15 us -> 12.9 us
    pallas_call x1, Pallas kernels: 99.7 us -> 96.5 us  [local(): pl.pallas_call(functools.partial(exchange, node_count, local_k, batch), i...]
    another operation x2 -> x0, local copies, waits for them, and re-layouts: 1.69 us -> none  [the longest x1 0.84 us: local(): jnp.repeat(sin_k.astype(jnp.float32), 2 * bands, axis=1)[:, None, :]]
where the time goes in v3:
time: 132 us; the launch traced here: 131 us
  Pallas kernels  112 us (85%)
  local copies, waits for them, and re-layouts  12.9 us (10%)
  other arithmetic  5.38 us (4%)
    pallas_call x1, Pallas kernels, local(): pl.pallas_call(functools.partial(exchange, node_count, local_k, batch), i...  96.5 us
    pallas_call x1, Pallas kernels, local(): pl.pallas_call(functools.partial(hand_over, node_count), in_specs=[vmem],...  15.5 us
    unnamed x17, local copies, waits for them, and re-layouts  2.9 us
    gather x1, local copies, waits for them, and re-layouts, local(): strength = state_rows[picked].reshape(-1, modes, bands)  2.73 us

profile of v3, /device:TPU:0, one launch (start us, length us, event | category | flops | bytes accessed | tf_op | source)
XLA Modules:
  0.0 131.2 jit_solution(4000999165101761463)
XLA Ops:
  0.6 0.0 copy-start
  0.6 0.9 slice_bitcast_fusion.7
  1.5 0.8 copy.97
  2.4 0.1 maximum_bitcast_fusion
  2.5 0.1 maximum_bitcast_fusion.1
  2.6 0.6 pad_maximum_fusion.packs_ref
  3.2 0.8 pad_add_fusion
  4.0 0.1 copy.96
  4.1 0.8 multiply_reduce_fusion.4
  4.9 0.1 fusion.28
  4.9 0.1 cosine_convert_fusion.1
  5.0 0.6 pad_maximum_fusion.2.mix_ref
  5.6 0.8 multiply_reduce_fusion.3
  6.4 0.1 cosine_convert_fusion
  6.5 0.1 copy.106
  6.5 0.2 broadcast_in_dim.31
  6.7 1.0 reshape.468.wave_ref
  7.7 0.0 copy-start.4
  7.7 96.5 %exchange.1 = bf16[2,4,32,3840]{3,2,1,0:T(8,128)(2,1)} custom-call(bf16[2,1,8,122880]{3,2,1,0:T(8,128)(2,1)} %x_ref.1, bf16[2,8,8]{2,1,0:T(8,128)(2,1)} %pad_maximum_fusion.2.mix_ref, bf16[4,2,120,120]{3,2,1,0:T(8,128)(2,1)} %evec_ref.1, bf16[4,2,32,128]{3,2,1,0:T(8,128)(2,1)} %pad_maximum_fusion.packs_ref, f32[32,2,1024]{2,1,0:T(2,128)} %reshape.468.wave_ref, ...), custom_call_target="tpu_custom_call" | custom-call | tf_op jit(solution)/shard_map/exchange/pallas_call | solution.py:561
  104.3 0.0 copy-done.4
  104.3 0.1 copy.107
  104.4 0.1 copy.108
  104.5 0.1 reshape.470
  104.7 2.7 %gather_fusion.1 = bf16[32,3840]{1,0:T(8,128)(2,1)S(1)} fusion(bf16[256,3840]{1,0:T(8,128)(2,1)} %bitcast.78, s32[1024]{0:T(1024)S(1)} %pad_clamp_fusion), kind=kCustom, calls=%fused_computation.1 | custom fusion | bytes 491648 | tf_op jit(solution)/shard_map/gather | solution.py:600
  107.4 0.0 copy-start.2
  107.4 0.6 reshape.474
  108.0 0.0 copy-start.3
  108.0 0.0 copy-start.5
  108.0 0.5 copy.109
  108.5 0.0 copy-start.1
  108.5 0.0 copy-done
  108.6 0.7 gather_fusion.3
  109.2 0.0 copy-done.2
  109.2 0.7 gather_fusion.2
  110.0 0.1 fusion.29
  110.0 0.0 copy-done.3
  110.0 0.6 gather_fusion
  110.6 0.8 multiply_reduce_fusion.1
  111.5 0.0 copy-done.5
  111.5 0.2 fusion.7
  111.7 0.2 fusion.6
  111.9 0.1 copy.112
  112.0 0.1 copy.113
  112.1 0.8 copy.116.value_ref
  112.9 15.5 %hand_over.1 = f32[8,128]{1,0:T(8,128)} custom-call(f32[16,8,128]{2,1,0:T(8,128)} %copy.116.value_ref), custom_call_target="tpu_custom_call" | custom-call | tf_op jit(solution)/shard_map/hand_over/pallas_call | solution.py:610
  128.5 0.7 slice_reduce_fusion
  129.2 0.1 reshape.473
  129.3 0.7 copy.115
  129.9 0.0 copy-done.1
  129.9 1.3 copy.129
  (19 shorter events, 0.2 us)
Async XLA Ops:
  0.6 107.9 %copy-start = (f32[32,4,32]{2,1,0:T(4,128)S(1)}, f32[32,4,32]{2,1,0:T(4,128)}, u32[]{:S(2)}) copy-start(f32[32,4,32]{2,1,0:T(4,128)} %param.24) | copy-start | bytes 49156
  7.7 96.6 %copy-start.4 = (s32[16,16]{1,0:T(8,128)S(1)}, s32[16,16]{1,0:T(8,128)}, u32[]{:S(2)}) copy-start(s32[16,16]{1,0:T(8,128)} %param.26) | copy-start | bytes 3076
  107.4 1.8 %copy-start.2 = (f32[32,32]{1,0:T(8,128)S(1)}, f32[32,32]{1,0:T(8,128)}, u32[]{:S(2)}) copy-start(f32[32,32]{1,0:T(8,128)} %param.23) | copy-start | bytes 12292
  108.0 2.1 %copy-start.3 = (f32[4,120]{1,0:T(4,128)S(1)}, f32[4,120]{1,0:T(4,128)}, u32[]{:S(2)}) copy-start(f32[4,120]{1,0:T(4,128)} %param.22) | copy-start | bytes 5764
  108.0 3.5 %copy-start.5 = (f32[8]{0:T(128)S(1)}, f32[8]{0:T(128)}, u32[]{:S(2)}) copy-start(f32[8]{0:T(128)} %param.25) | copy-start | bytes 100
  108.5 21.4 %copy-start.1 = (bf16[2,4,32,3840]{3,2,1,0:T(8,128)(2,1)S(1)}, bf16[2,4,32,3840]{3,2,1,0:T(8,128)(2,1)}, u32[]{:S(2)}) copy-start(bf16[2,4,32,3840]{3,2,1,0:T(8,128)(2,1)} %exchange.1) | copy-start | bytes 5898244
